TPU v7x, 32 devices: a whole 2x2x4 slice. The times are simulated.
32 devices in a mesh: section: 4 (over y, x), tensor: 8 (over z, core).
Axes of the slice: x: 2, y: 2, z: 4, core: 2. Of those that a mesh axis runs over, the one named last changes fastest.
Arguments:
- hidden: bfloat16 [512, 16384], P('section', 'tensor')
- norm_gain: float32 [16384], P('tensor'), may hold values from 0.3 to 3
- head_weight: bfloat16 [16384, 8192], P(None, ('section', 'tensor'))
- tile_list: int32 [512, 16], replicated, may hold values from 0 to 63, as said below
- tile_count: int32 [512], replicated, may hold values from 1 to 16, as said below
- chosen_token: int32 [512], replicated, may hold values from 0 to 8191, as said below
- chosen_embed: bfloat16 [512, 16384], P('section', 'tensor'), may hold values from -6 to 6
- stack_state: int32 [512], P('section'), may hold values from 0 to 511
- state_table: bfloat16 [512, 16384], P(None, 'tensor'), may hold values from -6 to 6
Outputs:
- log_prob: float32 [512], replicated
- normalizer: float32 [512], replicated
- next_input: bfloat16 [512, 16384], P('section', 'tensor')
Inputs may be any that keep to these rules, and one draw needn't show every extreme that they name: `tile_list`: each row lists 16 different tiles; the first tile_count of them are its allowed tiles, the rest are tiles it does not allow. `tile_count`: some row has 16 allowed tiles and some row one. `chosen_token`: each chosen token lies in one of its row's allowed tiles.
All inputs are finite; a program needn't handle non-finite values.
Results may differ from a plain program's by a relative error of at most 0.0035.
Values may be sent and summed in bfloat16 or wider, within the bound.
A program may use at most 64 MiB of HBM per device.

v0:
```python
import jax
import jax.numpy as jnp
from jax import lax
from jax.sharding import PartitionSpec as P

D = 16384
TILE = 128
TILES_DEV = 2


EPSILON = 1e-05
NEG_FILL = -1e30


def shifted_2(value, axis, steps):
    count = lax.axis_size(axis)
    pairs = [(source, (source + steps) % count) for source in range(count)]
    return lax.ppermute(value, axis, pairs)


def scale_rows(widened, squares_total, width, gain):
    factor = lax.rsqrt(squares_total / width + EPSILON)
    return (widened * factor[:, None] * gain[None, :]).astype(jnp.bfloat16)


def shards(
    hidden,
    norm_gain,
    head_weight,
    tile_list,
    tile_count,
    chosen_token,
    chosen_embed,
    stack_state,
    state_table,
):
    states = jnp.arange(state_table.shape[0], dtype=jnp.int32)
    one_hot = (stack_state[:, None] == states[None, :]).astype(jnp.bfloat16)
    state_rows = jnp.dot(one_hot, state_table, preferred_element_type=jnp.float32)
    merged = (chosen_embed.astype(jnp.float32) + state_rows).astype(jnp.bfloat16)
    next_input = shifted_2(merged, "section", 1)
    widened = hidden.astype(jnp.float32)
    squares_total = lax.psum(jnp.sum(widened * widened, axis=1), "tensor")
    normed = scale_rows(widened, squares_total, D, norm_gain)
    all_rows = lax.all_gather(normed, "section", axis=0, tiled=True)
    logits = jnp.dot(
        lax.all_gather(all_rows, "tensor", axis=1, tiled=True),
        head_weight,
        preferred_element_type=jnp.float32,
    )
    row_count = logits.shape[0]
    vocab_here = logits.shape[1]
    device = lax.axis_index("section") * lax.axis_size("tensor") + lax.axis_index("tensor")
    own_tiles = device * TILES_DEV + jnp.arange(TILES_DEV, dtype=jnp.int32)
    live_slot = jnp.arange(tile_list.shape[1], dtype=jnp.int32)[None, :] < tile_count[:, None]
    matches = (tile_list[:, :, None] == own_tiles[None, None, :]) & live_slot[:, :, None]
    allowed = jnp.any(matches, axis=1)
    blocks = logits.reshape(row_count, TILES_DEV, TILE)
    allowed_mask = jnp.broadcast_to(allowed[:, :, None], blocks.shape)
    local_top = jnp.max(jnp.where(allowed_mask, blocks, NEG_FILL), axis=(1, 2))
    column = chosen_token - device * vocab_here
    columns = jnp.arange(vocab_here, dtype=jnp.int32)
    picked = jnp.sum(jnp.where(columns[None, :] == column[:, None], logits, 0.0), axis=1)
    row_top = lax.pmax(local_top, ("section", "tensor"))
    shifted = jnp.where(allowed_mask, blocks - row_top[:, None, None], NEG_FILL)
    terms = jnp.sum(jnp.exp(shifted), axis=(1, 2))
    totals, chosen_logit = lax.psum((terms, picked), ("section", "tensor"))
    normalizer = row_top + jnp.log(totals)
    log_prob = chosen_logit - normalizer
    return (log_prob, normalizer, next_input)


def solution(mesh):
    placed = (
        P("section", "tensor"),
        P("tensor"),
        P(None, ("section", "tensor")),
        P(),
        P(),
        P(),
        P("section", "tensor"),
        P("section"),
        P(None, "tensor"),
    )
    return jax.shard_map(
        shards,
        mesh=mesh,
        in_specs=placed,
        out_specs=(P(), P(), P("section", "tensor")),
        check_vma=False,
    )
```

profile of v0, /device:TPU:0, one launch (start us, length us, event | category | flops | bytes accessed | tf_op | source)
XLA Modules:
  0.0 315.1 jit_solution(2685323007243486026)
XLA Ops:
  7.2 0.0 copy-start
  7.2 0.0 all-gather.3.cloned.1.call-start
  7.2 1.4 fusion.1
  8.6 18.1 %psum.21 = f32[128]{0:T(128)S(1)} all-reduce(f32[128]{0:T(128)S(1)} %fusion.1), channel_id=1, replica_groups=mesh['section'=4,'tensor'=8] {'tensor'}, use_global_device_ids=true, to_apply=%region_1.0 | all-reduce | flops 128 | bytes 1024 | tf_op jit(solution)/shard_map/psum | solution.py:43
  26.7 2.0 fusion.3
  28.7 0.0 all-gather.3.cloned.1.call-update
  28.7 0.0 all-gather.5.cloned.1.call-start
  28.8 33.6 %all-gather.3.cloned.1.call-done = bf16[512,2048]{1,0:T(8,128)(2,1)} async-done(((bf16[128,2048]{1,0:T(8,128)(2,1)}), bf16[512,2048]{1,0:T(8,128)(2,1)}) %all-gather.3.cloned.1.call-update) | async-done | bytes 2097168 | tf_op jit(solution)/shard_map/all_gather | solution.py:45
  62.4 0.0 all-gather.5.cloned.1.call-update
  62.4 0.0 copy-done
  62.4 1.5 fusion
  64.0 1.5 collective-permute-start
  65.5 0.7 iota_compare_fusion.3
  66.2 0.9 and_reduce_fusion
  67.0 0.7 broadcast_subtract_fusion
  67.7 10.9 %collective-permute-done = bf16[128,2048]{1,0:T(8,128)(2,1)S(1)} collective-permute-done((bf16[128,2048]{1,0:T(8,128)(2,1)S(1)}, bf16[128,2048]{1,0:T(8,128)(2,1)S(1)}, u32[]{:S(2)}, u32[]{:S(2)}) %collective-permute-start) | collective-permute-done | bytes 524320 | tf_op jit(solution)/shard_map/ppermute | solution.py:18
  78.6 136.5 %all-gather.5.cloned.1.call-done = bf16[512,16384]{1,0:T(8,128)(2,1)} async-done(((bf16[512,2048]{1,0:T(8,128)(2,1)}), bf16[512,16384]{1,0:T(8,128)(2,1)}) %all-gather.5.cloned.1.call-update) | async-done | bytes 16777232 | tf_op jit(solution)/shard_map/all_gather | solution.py:47
  215.1 12.3 %fusion.4 = (f32[512]{0:T(512)S(1)}, f32[512,256]{0,1:T(8,128)S(1)}) fusion(pred[512,2]{0,1:T(4,128)(4,1)S(1)} %and_reduce_fusion, bf16[512,16384]{1,0:T(8,128)(2,1)} %all-gather.5.cloned.1.call-done, bf16[16384,256]{1,0:T(8,128)(2,1)} %param.11), kind=kOutput, calls=%fused_computation.9 | convolution fusion | flops 4295228928 | bytes 25693184 | tf_op jit(solution)/shard_map/dot_general | solution.py:46
  227.5 38.4 %pmax.7 = f32[512]{0:T(512)S(1)} all-reduce(f32[512]{0:T(512)S(1)} %get-tuple-element.9), channel_id=1, replica_groups=mesh['section'=4,'tensor'=8] {'section','tensor'}, use_global_device_ids=true, to_apply=%region_6.7 | all-reduce | flops 512 | bytes 4096 | tf_op jit(solution)/shard_map/pmax | solution.py:64
  265.9 0.2 fusion.6
  266.1 40.9 %all-reduce = (f32[512]{0:T(512)S(1)}, f32[512]{0:T(512)S(1)}) all-reduce(f32[512]{0:T(512)S(1)} %get-tuple-element.4, f32[512]{0:T(512)S(1)} %get-tuple-element.3), channel_id=1, replica_groups=mesh['section'=4,'tensor'=8] {'section','tensor'}, use_global_device_ids=true, to_apply=%region_3.4 | all-reduce | flops 1024 | bytes 8192 | tf_op jit(solution)/shard_map/psum | solution.py:67
  306.9 0.6 fusion.8
  307.5 0.8 copy.14
  (2 shorter events, 0.0 us)
Async XLA Ops:
  7.2 55.3 %copy-start = (bf16[512,2048]{1,0:T(8,128)(2,1)S(1)}, bf16[512,2048]{1,0:T(8,128)(2,1)}, u32[]{:S(2)}) copy-start(bf16[512,2048]{1,0:T(8,128)(2,1)} %param.17) | copy-start | bytes 6291460
  7.2 55.2 %all-gather.3.cloned.1.call-start = ((), (), s32[]{:S(2)}) async-start(), calls=%async_computation | async-start | bytes 2621440 | tf_op jit(solution)/shard_map/all_gather | solution.py:45
  28.7 186.4 %all-gather.5.cloned.1.call-start = ((), (), s32[]{:S(2)}) async-start(), calls=%async_computation.1 | async-start | bytes 18874368 | tf_op jit(solution)/shard_map/all_gather | solution.py:47
  64.0 14.6 %collective-permute-start = (bf16[128,2048]{1,0:T(8,128)(2,1)S(1)}, bf16[128,2048]{1,0:T(8,128)(2,1)S(1)}, u32[]{:S(2)}, u32[]{:S(2)}) collective-permute-start(bf16[128,2048]{1,0:T(8,128)(2,1)S(1)} %fusion), channel_id=1, source_target_pairs={{0,8},{8,16},{16,24},{24,0},{1,9},{9,17},{17,25},{25,1},{2,10},{10... | collective-permute-start | bytes 1572872 | tf_op jit(solution)/shard_map/ppermute | solution.py:18
Sparse Core Ops, SparseCore 0:
  28.8 33.5 all-gather.2
  64.0 151.0 all-gather.4
where the time goes:
time: 316 us; the launch traced here: 315 us
  waiting for transfers between devices  181 us (57%)
  blocking collectives  97.4 us (31%)
  between operations  14.1 us (4%)
  matrix products  13.8 us (4%)
  other arithmetic  6.4 us (2%)
    all_gather x1, waiting for transfers between devices, shards(): lax.all_gather(all_rows, 'tensor', axis=1, tiled=True)  137 us
    psum x1, blocking collectives, shards(): totals, chosen_logit = lax.psum((terms, picked), ('section', 'tensor'))  40.9 us
    pmax x1, blocking collectives, shards(): row_top = lax.pmax(local_top, ('section', 'tensor'))  38.4 us
    all_gather x1, waiting for transfers between devices, shards(): all_rows = lax.all_gather(normed, 'section', axis=0, tiled=True)  33.6 us
    psum x1, blocking collectives, shards(): squares_total = lax.psum(jnp.sum(widened * widened, axis=1), 'tensor')  18.1 us
    dot_general x1, matrix products, shards(): jnp.dot(lax.all_gather(all_rows, 'tensor', axis=1, tiled=True), head_weig...  12.3 us
    ppermute x1, waiting for transfers between devices, shifted_2(): return lax.ppermute(value, axis, pairs)  10.9 us
  transfers between devices with their start and end apart: 3, of which 3 were waited for; matrix products, arithmetic and copies ran while one was open for 1% of the time, Pallas kernels for 0%

commit v1 on v0

--- a/solution.py
+++ b/solution.py
@@ -1,6 +1,10 @@
+import functools
+
 import jax
 import jax.numpy as jnp
 from jax import lax
+from jax.experimental import pallas as pl
+from jax.experimental.pallas import tpu as pltpu
 from jax.sharding import PartitionSpec as P
 
 D = 16384
@@ -70,6 +74,345 @@
     return (log_prob, normalizer, next_input)
 
 
+LOWEST = -3e38
+MESH = pl.DeviceIdType.MESH
+ANY = pl.BlockSpec(memory_space=pl.ANY)
+VMEM = pl.BlockSpec(memory_space=pltpu.VMEM)
+
+
+def head_kernel(
+    hidden_hbm,
+    gain_ref,
+    weight_hbm,
+    tiles_ref,
+    count_ref,
+    token_ref,
+    embed_hbm,
+    state_ref,
+    table_hbm,
+    log_prob_ref,
+    normalizer_ref,
+    next_hbm,
+    rows_all,
+    weight,
+    total,
+    hidden,
+    embed,
+    table,
+    merged,
+    parts,
+    plane_stats,
+    line_stats,
+    send_sems,
+    line_sems,
+    recv_sems,
+    next_sem,
+    parts_sems,
+    plane_sems,
+    line_stat_sems,
+    local_sems,
+):
+    section = lax.axis_index("section")
+    tensor = lax.axis_index("tensor")
+    sections = 4
+    tensors = 8
+    x, y = section % 2, section // 2
+    z, core = tensor // 2, tensor % 2
+    beside_x = section + 1 - 2 * x
+    beside_y = section + 2 - 4 * y
+    across = 3 - section
+    twin = tensor + 1 - 2 * core
+    height, width = hidden.shape
+    half = height // 2
+    columns = weight.shape[1]
+    device = section * tensors + tensor
+
+    reads = [
+        pltpu.make_async_copy(source, target, local_sems.at[n])
+        for n, (source, target) in enumerate(
+            ((hidden_hbm, hidden), (table_hbm, table), (embed_hbm, embed), (weight_hbm, weight))
+        )
+    ]
+    for read in reads:
+        read.start()
+
+    plane = [((section + k // 2) % sections, (tensor // 2) * 2 + (core + k) % 2) for k in range(1, 8)]
+    line = [(section, (tensor + k) % tensors) for k in range(1, 8)]
+    barrier = pltpu.get_barrier_semaphore()
+    greeted = plane + [(section, ((z + k) % 4) * 2 + c) for k in range(1, 4) for c in range(2)]
+    for peer in greeted:
+        pl.semaphore_signal(barrier, inc=1, device_id=peer, device_id_type=MESH)
+
+    reads[0].wait()
+    widened = hidden[...].astype(jnp.float32)
+    squares = jnp.sum(widened * widened, axis=1, keepdims=True)
+    laid = jnp.transpose(jnp.broadcast_to(squares, (height, 128)))[0:8, :]
+    parts[pl.ds(tensor, 1)] = laid[None]
+    pl.semaphore_wait(barrier, len(greeted))
+
+    unconditional = []
+    conditional = []
+
+    def push(source, target, receive, peer, when=None):
+        if when is None:
+            copy = pltpu.make_async_remote_copy(
+                src_ref=source,
+                dst_ref=target,
+                send_sem=send_sems.at[len(unconditional)],
+                recv_sem=receive,
+                device_id=peer,
+                device_id_type=MESH,
+            )
+            unconditional.append(copy)
+            copy.start()
+        else:
+            copy = pltpu.make_async_remote_copy(
+                src_ref=source,
+                dst_ref=target,
+                send_sem=line_sems.at[len(conditional)],
+                recv_sem=receive,
+                device_id=peer,
+                device_id_type=MESH,
+            )
+            conditional.append((when, copy))
+            pl.when(when)(copy.start)
+
+    def arrived(target, receive):
+        pltpu.make_async_remote_copy(
+            src_ref=target,
+            dst_ref=target,
+            send_sem=send_sems.at[0],
+            recv_sem=receive,
+            device_id=(section, twin),
+            device_id_type=MESH,
+        ).wait_recv()
+
+    for peer in line:
+        push(parts.at[tensor], parts.at[tensor], parts_sems.at[tensor], peer)
+
+    states = lax.broadcasted_iota(jnp.int32, (table.shape[0], height), 0)
+    one_hot = jnp.transpose((states == state_ref[...]).astype(jnp.float32)).astype(jnp.bfloat16)
+    reads[1].wait()
+    reads[2].wait()
+    state_rows = jnp.dot(one_hot, table[...], preferred_element_type=jnp.float32)
+    merged[...] = (embed[...].astype(jnp.float32) + state_rows).astype(jnp.bfloat16)
+    push(merged, next_hbm, next_sem, ((section + 1) % sections, tensor))
+
+    for _, peer in line:
+        arrived(parts.at[peer], parts_sems.at[peer])
+    squares_total = jnp.sum(parts[...], axis=0)[0:1, :]
+    factor = lax.rsqrt(squares_total / (width * tensors) + EPSILON)
+    factor = jnp.transpose(jnp.broadcast_to(factor, (128, height)))[:, 0:1]
+    own = section * tensors + tensor
+    rows_all[pl.ds(own, 1)] = (hidden[...].astype(jnp.float32) * factor * gain_ref[...]).astype(jnp.bfloat16)[None]
+
+    top, low = pl.ds(0, half), pl.ds(half, half)
+    total[...] = jnp.zeros_like(total)
+
+    def multiply(from_section, from_tensor):
+        row = pl.ds(pl.multiple_of(from_section * height, height), height)
+        feature = pl.ds(pl.multiple_of(from_tensor * width, width), width)
+        total[row, :] += jnp.dot(
+            rows_all[from_section * tensors + from_tensor], weight[feature, :], preferred_element_type=jnp.float32
+        )
+
+    upper = z // 2
+    order = []
+    mirrored = z + upper * (3 - 2 * z)
+    for place in (mirrored, 1 - mirrored, 2, 3):
+        order.append(place + upper * (3 - 2 * place))
+
+    def to_twin(block):
+        push(rows_all.at[block], rows_all.at[block], recv_sems.at[block, 0], (section, twin))
+
+    def from_line(step):
+        place = order[step]
+        block = section * tensors + place * 2 + core
+        whole = rows_all.at[block]
+        if step:
+            arrived(whole, recv_sems.at[block, 0])
+        push(whole, whole, recv_sems.at[block, 0], (section, tensor + 2), (place <= z) & (z < 3))
+        push(whole, whole, recv_sems.at[block, 0], (section, tensor - 2), (place >= z) & (z > 0))
+        for peer, parts_in_order in ((beside_x, (0, 1)), (beside_y, (1, 0))):
+            for part in parts_in_order:
+                piece = rows_all.at[block, (top, low)[part]]
+                push(piece, piece, recv_sems.at[block, part], (peer, tensor))
+        to_twin(block)
+        if step == 0:
+            reads[3].wait()
+        multiply(section, place * 2 + core)
+
+    def from_beside(step):
+        column = order[step] * 2 + core
+        for source, onward, part in ((beside_x, beside_y, 0), (beside_y, beside_x, 1)):
+            block = source * tensors + column
+            piece = rows_all.at[block, (top, low)[part]]
+            arrived(piece, recv_sems.at[block, part])
+            push(piece, piece, recv_sems.at[block, part], (onward, tensor))
+        for source, part in ((beside_x, 1), (beside_y, 0)):
+            block = source * tensors + column
+            piece = rows_all.at[block, (top, low)[part]]
+            arrived(piece, recv_sems.at[block, part])
+            to_twin(block)
+        multiply(beside_x, column)
+        multiply(beside_y, column)
+
+    def from_across(step):
+        column = order[step] * 2 + core
+        block = across * tensors + column
+        for part in range(2):
+            arrived(rows_all.at[block, (top, low)[part]], recv_sems.at[block, part])
+        to_twin(block)
+        multiply(across, column)
+
+    def from_twin(sources, step):
+        column = order[step] * 2 + 1 - core
+        for source in sources:
+            block = source * tensors + column
+            arrived(rows_all.at[block], recv_sems.at[block, 0])
+            multiply(source, column)
+
+    aside = (beside_x, beside_y)
+    from_line(0)
+    from_beside(0)
+    from_line(1)
+    from_twin((section,), 0)
+    from_twin(aside, 0)
+    from_across(0)
+    from_line(2)
+    from_twin((section,), 1)
+    from_twin((across,), 0)
+    from_beside(1)
+    from_line(3)
+    from_twin(aside, 1)
+    from_twin((section,), 2)
+    from_across(1)
+    from_beside(2)
+    from_twin((across,), 1)
+    from_twin((section,), 3)
+    from_twin(aside, 2)
+    from_across(2)
+    from_beside(3)
+    from_twin((across,), 2)
+    from_twin(aside, 3)
+    from_across(3)
+    from_twin((across,), 3)
+
+    logits = jnp.transpose(total[...])
+    slots = lax.broadcasted_iota(jnp.int32, tiles_ref.shape, 0)
+    live = slots < count_ref[...]
+    own_tiles = columns // TILE
+    hits = []
+    for n in range(own_tiles):
+        match = live & (tiles_ref[...] == device * own_tiles + n)
+        hits.append(jnp.max(match.astype(jnp.int32), axis=0, keepdims=True) > 0)
+    blocks = [logits[n * TILE:(n + 1) * TILE, :] for n in range(own_tiles)]
+    largest = jnp.full(count_ref.shape, LOWEST, jnp.float32)
+    for hit, block in zip(hits, blocks):
+        largest = jnp.maximum(largest, jnp.where(hit, jnp.max(block, axis=0, keepdims=True), LOWEST))
+    terms = jnp.zeros_like(largest)
+    for hit, block in zip(hits, blocks):
+        terms += jnp.where(hit, jnp.sum(jnp.exp(block - largest), axis=0, keepdims=True), 0.0)
+    place = lax.broadcasted_iota(jnp.int32, logits.shape, 0)
+    chosen = jnp.sum(jnp.where(place == token_ref[...] - device * columns, logits, 0.0), axis=0, keepdims=True)
+
+    def packed(largest, terms, chosen):
+        line = lax.broadcasted_iota(jnp.int32, (8, largest.shape[1]), 0)
+        return jnp.where(line == 0, largest, jnp.where(line == 1, terms, jnp.where(line == 2, chosen, 0.0)))
+
+    def combined(stats):
+        values = [stats[n] for n in range(stats.shape[0])]
+        largest = functools.reduce(jnp.maximum, [value[0:1, :] for value in values])
+        terms = sum(value[1:2, :] * jnp.exp(value[0:1, :] - largest) for value in values)
+        chosen = sum(value[2:3, :] for value in values)
+        return largest, terms, chosen
+
+    slot = section * 2 + core
+    plane_stats[pl.ds(slot, 1)] = packed(largest, terms, chosen)[None]
+    for peer in plane:
+        push(plane_stats.at[slot], plane_stats.at[slot], plane_sems.at[slot], peer)
+    for peer_section, peer_tensor in plane:
+        peer_slot = peer_section * 2 + peer_tensor % 2
+        arrived(plane_stats.at[peer_slot], plane_sems.at[peer_slot])
+    line_stats[pl.ds(z, 1)] = packed(*combined(plane_stats))[None]
+    for k in range(1, 4):
+        push(line_stats.at[z], line_stats.at[z], line_stat_sems.at[z], (section, ((z + k) % 4) * 2 + core))
+    for k in range(1, 4):
+        peer_z = (z + k) % 4
+        arrived(line_stats.at[peer_z], line_stat_sems.at[peer_z])
+    largest, terms, chosen = combined(line_stats)
+    normalizer = largest + jnp.log(terms)
+    normalizer_ref[...] = normalizer
+    log_prob_ref[...] = chosen - normalizer
+
+    arrived(next_hbm, next_sem)
+    for copy in unconditional:
+        copy.wait_send()
+    for when, copy in conditional:
+        pl.when(when)(copy.wait_send)
+
+
+def block_shards(
+    hidden,
+    norm_gain,
+    head_weight,
+    tile_list,
+    tile_count,
+    chosen_token,
+    chosen_embed,
+    stack_state,
+    state_table,
+):
+    height, width = hidden.shape
+    row_count = tile_count.shape[0]
+    dma = pltpu.SemaphoreType.DMA
+    log_prob, normalizer, next_input = pl.pallas_call(
+        head_kernel,
+        out_shape=(
+            jax.ShapeDtypeStruct((1, row_count), jnp.float32),
+            jax.ShapeDtypeStruct((1, row_count), jnp.float32),
+            jax.ShapeDtypeStruct(chosen_embed.shape, jnp.bfloat16),
+        ),
+        in_specs=[ANY, VMEM, ANY, VMEM, VMEM, VMEM, ANY, VMEM, ANY],
+        out_specs=(VMEM, VMEM, ANY),
+        scratch_shapes=[
+            pltpu.VMEM((32, height, width), jnp.bfloat16),
+            pltpu.VMEM(head_weight.shape, jnp.bfloat16),
+            pltpu.VMEM((row_count, head_weight.shape[1]), jnp.float32),
+            pltpu.VMEM(hidden.shape, jnp.bfloat16),
+            pltpu.VMEM(chosen_embed.shape, jnp.bfloat16),
+            pltpu.VMEM(state_table.shape, jnp.bfloat16),
+            pltpu.VMEM(chosen_embed.shape, jnp.bfloat16),
+            pltpu.VMEM((8, 8, height), jnp.float32),
+            pltpu.VMEM((8, 8, row_count), jnp.float32),
+            pltpu.VMEM((4, 8, row_count), jnp.float32),
+            dma((80,)),
+            dma((8,)),
+            dma((32, 2)),
+            dma,
+            dma((8,)),
+            dma((8,)),
+            dma((4,)),
+            dma((4,)),
+        ],
+        compiler_params=pltpu.CompilerParams(
+            collective_id=0, has_side_effects=True, vmem_limit_bytes=48 * 1024 * 1024
+        ),
+        name="masked_head",
+    )(
+        hidden,
+        norm_gain[None, :],
+        head_weight,
+        tile_list.T,
+        tile_count[None, :],
+        chosen_token[None, :],
+        chosen_embed,
+        stack_state[None, :],
+        state_table,
+    )
+    return (log_prob[0], normalizer[0], next_input)
+
+
 def solution(mesh):
     placed = (
         P("section", "tensor"),
@@ -82,8 +425,9 @@
         P("section"),
         P(None, "tensor"),
     )
+    small = mesh.shape["section"] == 4 and mesh.shape["tensor"] == 8
     return jax.shard_map(
-        shards,
+        block_shards if small else shards,
         mesh=mesh,
         in_specs=placed,
         out_specs=(P(), P(), P("section", "tensor")),

time: 316 us -> 113 us (0.36)
  waiting for transfers between devices: 181 us -> 0 us
  Pallas kernels: 0 us -> 103 us
  blocking collectives: 97.4 us -> 0 us
  matrix products: 13.8 us -> 0 us
  between operations: 14.1 us -> 0.66 us
  local copies, waits for them, and re-layouts: 0.8 us -> 9.09 us
  other arithmetic: 6.4 us -> 0 us
    all_gather x2 -> x0, waiting for transfers between devices: 170 us -> none  [the longest x1 137 us: shards(): lax.all_gather(all_rows, 'tensor', axis=1, tiled=True)]
    pallas_call x0 -> x1, Pallas kernels: none -> 103 us  [block_shards(): pl.pallas_call(head_kernel, out_shape=(jax.ShapeDtypeStruct((1, row_count...]
    psum x2 -> x0, blocking collectives: 58.9 us -> none  [the longest x1 40.9 us: shards(): totals, chosen_logit = lax.psum((terms, picked), ('section', 'tensor'))]
    pmax x1 -> x0, blocking collectives: 38.4 us -> none  [shards(): row_top = lax.pmax(local_top, ('section', 'tensor'))]
    dot_general x2 -> x0, matrix products: 13.8 us -> none  [the longest x1 12.3 us: shards(): jnp.dot(lax.all_gather(all_rows, 'tensor', axis=1, tiled=True), head_weig...]
    ppermute x1 -> x0, waiting for transfers between devices: 10.9 us -> none  [shifted_2(): return lax.ppermute(value, axis, pairs)]
    unnamed x3 -> x19, local copies, waits for them, and re-layouts: 0.8 us -> 9.09 us
  transfers between devices with their start and end apart: 3 -> 0, of which waited for: 3 -> 0; matrix products, arithmetic and copies ran while one was open for 1% -> 0% of each run, Pallas kernels for 0% -> 0%
where the time goes in v1:
time: 113 us
  Pallas kernels  103 us (91%)
  local copies, waits for them, and re-layouts  9.09 us (8%)
    pallas_call x1, Pallas kernels, block_shards(): pl.pallas_call(head_kernel, out_shape=(jax.ShapeDtypeStruct((1, row_count...  103 us
    unnamed x19, local copies, waits for them, and re-layouts  9.09 us

profile of v1, /device:TPU:0, one launch (start us, length us, event | category | flops | bytes accessed | tf_op | source)
XLA Modules:
  0.0 112.7 jit_solution(1614596023263797754)
XLA Ops:
  0.6 0.0 copy-start
  0.6 1.6 %copy-done = bf16[512,2048]{1,0:T(8,128)(2,1)S(1)} copy-done((bf16[512,2048]{1,0:T(8,128)(2,1)S(1)}, bf16[512,2048]{1,0:T(8,128)(2,1)}, u32[]{:S(2)}) %copy-start) | copy-done | bytes 2097176
  2.2 0.0 copy-start.1
  2.2 1.0 copy-done.1
  3.3 0.0 copy-start.2
  3.3 1.0 copy-done.2
  4.3 0.0 copy-start.3
  4.3 0.8 copy-done.3
  5.1 0.0 copy-start.4
  5.1 0.7 copy-done.4
  5.8 0.0 copy-start.5
  5.8 0.7 copy-done.5
  6.4 0.0 copy-start.6
  6.5 0.7 copy-done.6
  7.1 0.0 copy-start.7
  7.1 0.7 copy-done.7
  7.8 103.0 %masked_head.1 = (f32[1,512]{1,0:T(1,128)S(1)}, f32[1,512]{1,0:T(1,128)S(1)}, bf16[128,2048]{1,0:T(8,128)(2,1)S(1)}) custom-call(bf16[128,2048]{1,0:T(8,128)(2,1)S(1)} %copy-done.1, f32[1,2048]{1,0:T(1,128)S(1)} %bitcast.8, bf16[16384,256]{1,0:T(8,128)(2,1)} %weight_hbm.1, s32[16,512]{1,0:T(8,128)S(1)} %bitcast.7, s32[1,512]{1,0:T(1,128)S(1)} %bitcast.9, ...), custom_call_target="tpu_custom_call" | custom-call | tf_op jit(solution)/shard_map/masked_head/pallas_call | solution.py:369
  110.8 0.6 copy.15
  111.4 0.6 copy.16
  111.9 0.8 copy.17
Async XLA Ops:
  0.6 1.6 %copy-start = (bf16[512,2048]{1,0:T(8,128)(2,1)S(1)}, bf16[512,2048]{1,0:T(8,128)(2,1)}, u32[]{:S(2)}) copy-start(bf16[512,2048]{1,0:T(8,128)(2,1)} %table_hbm.1) | copy-start | bytes 6291460
  2.2 1.0 copy-start.1
  3.3 1.0 copy-start.2
  4.3 0.8 copy-start.3
  5.1 0.7 copy-start.4
  5.8 0.7 copy-start.5
  6.4 0.7 copy-start.6
  7.1 0.7 copy-start.7

commit v2 on v1

--- a/solution.py
+++ b/solution.py
@@ -76,19 +76,19 @@
 
 LOWEST = -3e38
 MESH = pl.DeviceIdType.MESH
-ANY = pl.BlockSpec(memory_space=pl.ANY)
+HBM = pl.BlockSpec(memory_space=pltpu.HBM)
 VMEM = pl.BlockSpec(memory_space=pltpu.VMEM)
 
 
 def head_kernel(
     hidden_hbm,
-    gain_ref,
+    gain_hbm,
     weight_hbm,
-    tiles_ref,
-    count_ref,
-    token_ref,
+    tiles_hbm,
+    count_hbm,
+    token_hbm,
     embed_hbm,
-    state_ref,
+    state_hbm,
     table_hbm,
     log_prob_ref,
     normalizer_ref,
@@ -100,6 +100,11 @@
     embed,
     table,
     merged,
+    gain_ref,
+    tiles_ref,
+    count_ref,
+    token_ref,
+    state_ref,
     parts,
     plane_stats,
     line_stats,
@@ -123,14 +128,23 @@
     across = 3 - section
     twin = tensor + 1 - 2 * core
     height, width = hidden.shape
-    half = height // 2
     columns = weight.shape[1]
     device = section * tensors + tensor
 
     reads = [
         pltpu.make_async_copy(source, target, local_sems.at[n])
         for n, (source, target) in enumerate(
-            ((hidden_hbm, hidden), (table_hbm, table), (embed_hbm, embed), (weight_hbm, weight))
+            (
+                (hidden_hbm, hidden),
+                (table_hbm, table),
+                (embed_hbm, embed),
+                (weight_hbm, weight),
+                (state_hbm, state_ref),
+                (gain_hbm, gain_ref),
+                (tiles_hbm, tiles_ref),
+                (count_hbm, count_ref),
+                (token_hbm, token_ref),
+            )
         )
     ]
     for read in reads:
@@ -190,6 +204,7 @@
     for peer in line:
         push(parts.at[tensor], parts.at[tensor], parts_sems.at[tensor], peer)
 
+    reads[4].wait()
     states = lax.broadcasted_iota(jnp.int32, (table.shape[0], height), 0)
     one_hot = jnp.transpose((states == state_ref[...]).astype(jnp.float32)).astype(jnp.bfloat16)
     reads[1].wait()
@@ -201,12 +216,19 @@
     for _, peer in line:
         arrived(parts.at[peer], parts_sems.at[peer])
     squares_total = jnp.sum(parts[...], axis=0)[0:1, :]
+    reads[5].wait()
     factor = lax.rsqrt(squares_total / (width * tensors) + EPSILON)
     factor = jnp.transpose(jnp.broadcast_to(factor, (128, height)))[:, 0:1]
     own = section * tensors + tensor
     rows_all[pl.ds(own, 1)] = (hidden[...].astype(jnp.float32) * factor * gain_ref[...]).astype(jnp.bfloat16)[None]
 
-    top, low = pl.ds(0, half), pl.ds(half, half)
+    first = height * 3 // 4
+    tail = pl.ds(first, height - first)
+
+    def halves(step):
+        size = (first if step else height) // 2
+        return pl.ds(0, size), pl.ds(size, size)
+
     total[...] = jnp.zeros_like(total)
 
     def multiply(from_section, from_tensor):
@@ -225,34 +247,47 @@
     def to_twin(block):
         push(rows_all.at[block], rows_all.at[block], recv_sems.at[block, 0], (section, twin))
 
+    def along(piece, receive, place):
+        push(piece, piece, receive, (section, tensor + 2), (place <= z) & (z < 3))
+        push(piece, piece, receive, (section, tensor - 2), (place >= z) & (z > 0))
+
     def from_line(step):
         place = order[step]
         block = section * tensors + place * 2 + core
         whole = rows_all.at[block]
         if step:
             arrived(whole, recv_sems.at[block, 0])
-        push(whole, whole, recv_sems.at[block, 0], (section, tensor + 2), (place <= z) & (z < 3))
-        push(whole, whole, recv_sems.at[block, 0], (section, tensor - 2), (place >= z) & (z > 0))
+        along(whole, recv_sems.at[block, 0], place)
         for peer, parts_in_order in ((beside_x, (0, 1)), (beside_y, (1, 0))):
             for part in parts_in_order:
-                piece = rows_all.at[block, (top, low)[part]]
+                piece = rows_all.at[block, halves(step)[part]]
                 push(piece, piece, recv_sems.at[block, part], (peer, tensor))
         to_twin(block)
         if step == 0:
             reads[3].wait()
         multiply(section, place * 2 + core)
 
+    def tails(sources, step):
+        for source in sources:
+            block = source * tensors + order[step] * 2 + core
+            piece = rows_all.at[block, tail]
+            if step:
+                arrived(piece, recv_sems.at[block, 2])
+            along(piece, recv_sems.at[block, 2], order[step])
+
     def from_beside(step):
         column = order[step] * 2 + core
         for source, onward, part in ((beside_x, beside_y, 0), (beside_y, beside_x, 1)):
             block = source * tensors + column
-            piece = rows_all.at[block, (top, low)[part]]
+            piece = rows_all.at[block, halves(step)[part]]
             arrived(piece, recv_sems.at[block, part])
             push(piece, piece, recv_sems.at[block, part], (onward, tensor))
         for source, part in ((beside_x, 1), (beside_y, 0)):
             block = source * tensors + column
-            piece = rows_all.at[block, (top, low)[part]]
+            piece = rows_all.at[block, halves(step)[part]]
             arrived(piece, recv_sems.at[block, part])
+            if step == 0:
+                tails((source,), 0)
             to_twin(block)
         multiply(beside_x, column)
         multiply(beside_y, column)
@@ -261,7 +296,9 @@
         column = order[step] * 2 + core
         block = across * tensors + column
         for part in range(2):
-            arrived(rows_all.at[block, (top, low)[part]], recv_sems.at[block, part])
+            arrived(rows_all.at[block, halves(step)[part]], recv_sems.at[block, part])
+        if step == 0:
+            tails((across,), 0)
         to_twin(block)
         multiply(across, column)
 
@@ -273,31 +310,37 @@
             multiply(source, column)
 
     aside = (beside_x, beside_y)
+    others = (beside_x, beside_y, across)
     from_line(0)
     from_beside(0)
     from_line(1)
+    from_across(0)
     from_twin((section,), 0)
+    from_line(2)
+    tails(others, 1)
     from_twin(aside, 0)
-    from_across(0)
-    from_line(2)
+    from_beside(1)
     from_twin((section,), 1)
     from_twin((across,), 0)
-    from_beside(1)
     from_line(3)
+    tails(others, 2)
+    from_across(1)
+    from_twin((section,), 2)
     from_twin(aside, 1)
-    from_twin((section,), 2)
-    from_across(1)
     from_beside(2)
+    tails(others, 3)
     from_twin((across,), 1)
     from_twin((section,), 3)
+    from_across(2)
     from_twin(aside, 2)
-    from_across(2)
     from_beside(3)
     from_twin((across,), 2)
     from_twin(aside, 3)
     from_across(3)
     from_twin((across,), 3)
 
+    for read in reads[6:]:
+        read.wait()
     logits = jnp.transpose(total[...])
     slots = lax.broadcasted_iota(jnp.int32, tiles_ref.shape, 0)
     live = slots < count_ref[...]
@@ -373,8 +416,8 @@
             jax.ShapeDtypeStruct((1, row_count), jnp.float32),
             jax.ShapeDtypeStruct(chosen_embed.shape, jnp.bfloat16),
         ),
-        in_specs=[ANY, VMEM, ANY, VMEM, VMEM, VMEM, ANY, VMEM, ANY],
-        out_specs=(VMEM, VMEM, ANY),
+        in_specs=[HBM] * 9,
+        out_specs=(VMEM, VMEM, HBM),
         scratch_shapes=[
             pltpu.VMEM((32, height, width), jnp.bfloat16),
             pltpu.VMEM(head_weight.shape, jnp.bfloat16),
@@ -383,20 +426,25 @@
             pltpu.VMEM(chosen_embed.shape, jnp.bfloat16),
             pltpu.VMEM(state_table.shape, jnp.bfloat16),
             pltpu.VMEM(chosen_embed.shape, jnp.bfloat16),
+            pltpu.VMEM((1, width), jnp.float32),
+            pltpu.VMEM(tile_list.shape[::-1], jnp.int32),
+            pltpu.VMEM((1, row_count), jnp.int32),
+            pltpu.VMEM((1, row_count), jnp.int32),
+            pltpu.VMEM((1, height), jnp.int32),
             pltpu.VMEM((8, 8, height), jnp.float32),
             pltpu.VMEM((8, 8, row_count), jnp.float32),
             pltpu.VMEM((4, 8, row_count), jnp.float32),
             dma((80,)),
-            dma((8,)),
-            dma((32, 2)),
+            dma((32,)),
+            dma((32, 3)),
             dma,
             dma((8,)),
             dma((8,)),
             dma((4,)),
-            dma((4,)),
+            dma((9,)),
         ],
         compiler_params=pltpu.CompilerParams(
-            collective_id=0, has_side_effects=True, vmem_limit_bytes=48 * 1024 * 1024
+            collective_id=0, has_side_effects=True, vmem_limit_bytes=60 * 1024 * 1024
         ),
         name="masked_head",
     )(

time: 113 us -> 107 us (0.947)
  local copies, waits for them, and re-layouts: 9.09 us -> 4.38 us
    unnamed x19 -> x3, local copies, waits for them, and re-layouts: 9.09 us -> 4.38 us
where the time goes in v2:
time: 107 us
  Pallas kernels  102 us (95%)
  local copies, waits for them, and re-layouts  4.38 us (4%)
    pallas_call x1, Pallas kernels, block_shards(): pl.pallas_call(head_kernel, out_shape=(jax.ShapeDtypeStruct((1, row_count...  102 us
    unnamed x3, local copies, waits for them, and re-layouts  4.38 us

profile of v2, /device:TPU:0, one launch (start us, length us, event | category | flops | bytes accessed | tf_op | source)
XLA Modules:
  0.0 107.1 jit_solution(13945155562826912907)
XLA Ops:
  0.6 102.1 %masked_head.1 = (f32[1,512]{1,0:T(1,128)}, f32[1,512]{1,0:T(1,128)}, bf16[128,2048]{1,0:T(8,128)(2,1)}) custom-call(bf16[128,2048]{1,0:T(8,128)(2,1)} %hidden_hbm.1, f32[1,2048]{1,0:T(1,128)} %bitcast.8, bf16[16384,256]{1,0:T(8,128)(2,1)} %weight_hbm.1, s32[16,512]{1,0:T(8,128)} %bitcast.7, s32[1,512]{1,0:T(1,128)} %bitcast.9, s32[1,512]{1,0:T(1,128)} %bitcast.10, ...), custom_call_target="tpu_custom_call" | custom-call | tf_op jit(solution)/shard_map/masked_head/pallas_call | solution.py:412
  102.8 1.3 %copy.15 = f32[512]{0:T(512)} copy(f32[512]{0:T(512)} %bitcast.12) | data formatting | bytes 4096
  104.0 1.2 %copy.16 = f32[512]{0:T(512)} copy(f32[512]{0:T(512)} %bitcast.11) | data formatting | bytes 4096
  105.3 1.9 %copy.17 = bf16[128,2048]{1,0:T(8,128)(2,1)} copy(bf16[128,2048]{1,0:T(8,128)(2,1)} %get-tuple-element.14) | data formatting | bytes 1048576

commit v3 on v2

--- a/solution.py
+++ b/solution.py
@@ -77,6 +77,7 @@
 LOWEST = -3e38
 MESH = pl.DeviceIdType.MESH
 HBM = pl.BlockSpec(memory_space=pltpu.HBM)
+ANY = pl.BlockSpec(memory_space=pl.ANY)
 VMEM = pl.BlockSpec(memory_space=pltpu.VMEM)
 
 
@@ -95,7 +96,10 @@
     next_hbm,
     rows_all,
     weight,
+    twin_weight,
     total,
+    twin_total,
+    from_twin,
     hidden,
     embed,
     table,
@@ -111,6 +115,8 @@
     send_sems,
     line_sems,
     recv_sems,
+    weight_sems,
+    total_sems,
     next_sem,
     parts_sems,
     plane_sems,
@@ -128,7 +134,7 @@
     across = 3 - section
     twin = tensor + 1 - 2 * core
     height, width = hidden.shape
-    columns = weight.shape[1]
+    columns = weight.shape[2]
     device = section * tensors + tensor
 
     reads = [
@@ -138,7 +144,6 @@
                 (hidden_hbm, hidden),
                 (table_hbm, table),
                 (embed_hbm, embed),
-                (weight_hbm, weight),
                 (state_hbm, state_ref),
                 (gain_hbm, gain_ref),
                 (tiles_hbm, tiles_ref),
@@ -147,7 +152,22 @@
             )
         )
     ]
+    upper = z // 2
+    order = []
+    mirrored = z + upper * (3 - 2 * z)
+    for place in (mirrored, 1 - mirrored, 2, 3):
+        order.append(place + upper * (3 - 2 * place))
+
+    def features(place, of_core):
+        return pl.ds(pl.multiple_of((place * 2 + of_core) * width, width), width)
+
     for read in reads:
+        read.start()
+    weight_reads = [
+        pltpu.make_async_copy(weight_hbm.at[features(place, core)], weight.at[place], local_sems.at[len(reads) + n])
+        for n, place in enumerate(order)
+    ]
+    for read in weight_reads:
         read.start()
 
     plane = [((section + k // 2) % sections, (tensor // 2) * 2 + (core + k) % 2) for k in range(1, 8)]
@@ -201,10 +221,15 @@
             device_id_type=MESH,
         ).wait_recv()
 
+    def send_weight(step):
+        place = order[step]
+        source = weight_hbm.at[features(place, 1 - core)]
+        push(source, twin_weight.at[place], weight_sems.at[place], (section, twin))
+
     for peer in line:
         push(parts.at[tensor], parts.at[tensor], parts_sems.at[tensor], peer)
 
-    reads[4].wait()
+    reads[3].wait()
     states = lax.broadcasted_iota(jnp.int32, (table.shape[0], height), 0)
     one_hot = jnp.transpose((states == state_ref[...]).astype(jnp.float32)).astype(jnp.bfloat16)
     reads[1].wait()
@@ -213,13 +238,15 @@
     merged[...] = (embed[...].astype(jnp.float32) + state_rows).astype(jnp.bfloat16)
     push(merged, next_hbm, next_sem, ((section + 1) % sections, tensor))
 
+    send_weight(0)
+
     for _, peer in line:
         arrived(parts.at[peer], parts_sems.at[peer])
     squares_total = jnp.sum(parts[...], axis=0)[0:1, :]
-    reads[5].wait()
+    reads[4].wait()
     factor = lax.rsqrt(squares_total / (width * tensors) + EPSILON)
     factor = jnp.transpose(jnp.broadcast_to(factor, (128, height)))[:, 0:1]
-    own = section * tensors + tensor
+    own = section * 4 + z
     rows_all[pl.ds(own, 1)] = (hidden[...].astype(jnp.float32) * factor * gain_ref[...]).astype(jnp.bfloat16)[None]
 
     first = height * 3 // 4
@@ -229,23 +256,21 @@
         size = (first if step else height) // 2
         return pl.ds(0, size), pl.ds(size, size)
 
-    total[...] = jnp.zeros_like(total)
-
-    def multiply(from_section, from_tensor):
-        row = pl.ds(pl.multiple_of(from_section * height, height), height)
-        feature = pl.ds(pl.multiple_of(from_tensor * width, width), width)
-        total[row, :] += jnp.dot(
-            rows_all[from_section * tensors + from_tensor], weight[feature, :], preferred_element_type=jnp.float32
-        )
-
-    upper = z // 2
-    order = []
-    mirrored = z + upper * (3 - 2 * z)
-    for place in (mirrored, 1 - mirrored, 2, 3):
-        order.append(place + upper * (3 - 2 * place))
-
-    def to_twin(block):
-        push(rows_all.at[block], rows_all.at[block], recv_sems.at[block, 0], (section, twin))
+    def multiply(source, step):
+        place = order[step]
+        row = pl.ds(pl.multiple_of(source * height, height), height)
+        block = rows_all[source * 4 + place]
+        for sums, by in ((twin_total, twin_weight), (total, weight)):
+            product = jnp.dot(block, by[place], preferred_element_type=jnp.float32)
+            if step:
+                product += sums[row, :]
+            sums[row, :] = product
+        if step == 3:
+            push(twin_total.at[row], from_twin.at[row], total_sems.at[source], (section, twin))
+
+    def weights_there(step):
+        weight_reads[step].wait()
+        arrived(twin_weight.at[order[step]], weight_sems.at[order[step]])
 
     def along(piece, receive, place):
         push(piece, piece, receive, (section, tensor + 2), (place <= z) & (z < 3))
@@ -253,7 +278,7 @@
 
     def from_line(step):
         place = order[step]
-        block = section * tensors + place * 2 + core
+        block = section * 4 + place
         whole = rows_all.at[block]
         if step:
             arrived(whole, recv_sems.at[block, 0])
@@ -262,86 +287,66 @@
             for part in parts_in_order:
                 piece = rows_all.at[block, halves(step)[part]]
                 push(piece, piece, recv_sems.at[block, part], (peer, tensor))
-        to_twin(block)
         if step == 0:
-            reads[3].wait()
-        multiply(section, place * 2 + core)
+            for later in range(1, 4):
+                send_weight(later)
+        weights_there(step)
+        multiply(section, step)
 
     def tails(sources, step):
         for source in sources:
-            block = source * tensors + order[step] * 2 + core
+            block = source * 4 + order[step]
             piece = rows_all.at[block, tail]
             if step:
                 arrived(piece, recv_sems.at[block, 2])
             along(piece, recv_sems.at[block, 2], order[step])
 
     def from_beside(step):
-        column = order[step] * 2 + core
         for source, onward, part in ((beside_x, beside_y, 0), (beside_y, beside_x, 1)):
-            block = source * tensors + column
+            block = source * 4 + order[step]
             piece = rows_all.at[block, halves(step)[part]]
             arrived(piece, recv_sems.at[block, part])
             push(piece, piece, recv_sems.at[block, part], (onward, tensor))
         for source, part in ((beside_x, 1), (beside_y, 0)):
-            block = source * tensors + column
+            block = source * 4 + order[step]
             piece = rows_all.at[block, halves(step)[part]]
             arrived(piece, recv_sems.at[block, part])
             if step == 0:
                 tails((source,), 0)
-            to_twin(block)
-        multiply(beside_x, column)
-        multiply(beside_y, column)
+        multiply(beside_x, step)
+        multiply(beside_y, step)
 
     def from_across(step):
-        column = order[step] * 2 + core
-        block = across * tensors + column
+        block = across * 4 + order[step]
         for part in range(2):
             arrived(rows_all.at[block, halves(step)[part]], recv_sems.at[block, part])
         if step == 0:
             tails((across,), 0)
-        to_twin(block)
-        multiply(across, column)
-
-    def from_twin(sources, step):
-        column = order[step] * 2 + 1 - core
-        for source in sources:
-            block = source * tensors + column
-            arrived(rows_all.at[block], recv_sems.at[block, 0])
-            multiply(source, column)
-
-    aside = (beside_x, beside_y)
+        multiply(across, step)
+
     others = (beside_x, beside_y, across)
     from_line(0)
     from_beside(0)
     from_line(1)
     from_across(0)
-    from_twin((section,), 0)
     from_line(2)
     tails(others, 1)
-    from_twin(aside, 0)
     from_beside(1)
-    from_twin((section,), 1)
-    from_twin((across,), 0)
     from_line(3)
     tails(others, 2)
     from_across(1)
-    from_twin((section,), 2)
-    from_twin(aside, 1)
     from_beside(2)
     tails(others, 3)
-    from_twin((across,), 1)
-    from_twin((section,), 3)
     from_across(2)
-    from_twin(aside, 2)
     from_beside(3)
-    from_twin((across,), 2)
-    from_twin(aside, 3)
     from_across(3)
-    from_twin((across,), 3)
-
-    for read in reads[6:]:
+
+    for read in reads[5:]:
         read.wait()
-    logits = jnp.transpose(total[...])
+    for source in (section, *others):
+        row = pl.ds(pl.multiple_of(source * height, height), height)
+        arrived(from_twin.at[row], total_sems.at[source])
+    logits = jnp.transpose(total[...] + from_twin[...])
     slots = lax.broadcasted_iota(jnp.int32, tiles_ref.shape, 0)
     live = slots < count_ref[...]
     own_tiles = columns // TILE
@@ -408,6 +413,7 @@
 ):
     height, width = hidden.shape
     row_count = tile_count.shape[0]
+    columns = head_weight.shape[1]
     dma = pltpu.SemaphoreType.DMA
     log_prob, normalizer, next_input = pl.pallas_call(
         head_kernel,
@@ -417,11 +423,14 @@
             jax.ShapeDtypeStruct(chosen_embed.shape, jnp.bfloat16),
         ),
         in_specs=[HBM] * 9,
-        out_specs=(VMEM, VMEM, HBM),
+        out_specs=(VMEM, VMEM, ANY),
         scratch_shapes=[
-            pltpu.VMEM((32, height, width), jnp.bfloat16),
-            pltpu.VMEM(head_weight.shape, jnp.bfloat16),
-            pltpu.VMEM((row_count, head_weight.shape[1]), jnp.float32),
+            pltpu.VMEM((16, height, width), jnp.bfloat16),
+            pltpu.VMEM((4, width, columns), jnp.bfloat16),
+            pltpu.VMEM((4, width, columns), jnp.bfloat16),
+            pltpu.VMEM((row_count, columns), jnp.float32),
+            pltpu.VMEM((row_count, columns), jnp.float32),
+            pltpu.VMEM((row_count, columns), jnp.float32),
             pltpu.VMEM(hidden.shape, jnp.bfloat16),
             pltpu.VMEM(chosen_embed.shape, jnp.bfloat16),
             pltpu.VMEM(state_table.shape, jnp.bfloat16),
@@ -436,12 +445,14 @@
             pltpu.VMEM((4, 8, row_count), jnp.float32),
             dma((80,)),
             dma((32,)),
-            dma((32, 3)),
+            dma((16, 3)),
+            dma((4,)),
+            dma((4,)),
             dma,
             dma((8,)),
             dma((8,)),
             dma((4,)),
-            dma((9,)),
+            dma((12,)),
         ],
         compiler_params=pltpu.CompilerParams(
             collective_id=0, has_side_effects=True, vmem_limit_bytes=60 * 1024 * 1024

time: 107 us -> 103 us (0.963)
  Pallas kernels: 102 us -> 97.5 us
    pallas_call x1, Pallas kernels: 102 us -> 97.5 us  [block_shards(): pl.pallas_call(head_kernel, out_shape=(jax.ShapeDtypeStruct((1, row_count...]
where the time goes in v3:
time: 103 us
  Pallas kernels  97.5 us (95%)
  local copies, waits for them, and re-layouts  4.38 us (4%)
    pallas_call x1, Pallas kernels, block_shards(): pl.pallas_call(head_kernel, out_shape=(jax.ShapeDtypeStruct((1, row_count...  97.5 us
    unnamed x3, local copies, waits for them, and re-layouts  4.38 us

profile of v3, /device:TPU:0, one launch (start us, length us, event | category | flops | bytes accessed | tf_op | source)
XLA Modules:
  0.0 102.6 jit_solution(13796337841305635570)
XLA Ops:
  0.6 97.5 %masked_head.1 = (f32[1,512]{1,0:T(1,128)}, f32[1,512]{1,0:T(1,128)}, bf16[128,2048]{1,0:T(8,128)(2,1)}) custom-call(bf16[128,2048]{1,0:T(8,128)(2,1)} %hidden_hbm.1, f32[1,2048]{1,0:T(1,128)} %bitcast.8, bf16[16384,256]{1,0:T(8,128)(2,1)} %weight_hbm.1, s32[16,512]{1,0:T(8,128)} %bitcast.7, s32[1,512]{1,0:T(1,128)} %bitcast.9, s32[1,512]{1,0:T(1,128)} %bitcast.10, ...), custom_call_target="tpu_custom_call" | custom-call | tf_op jit(solution)/shard_map/masked_head/pallas_call | solution.py:418
  98.2 1.3 %copy.15 = f32[512]{0:T(512)} copy(f32[512]{0:T(512)} %bitcast.12) | data formatting | bytes 4096
  99.4 1.2 %copy.16 = f32[512]{0:T(512)} copy(f32[512]{0:T(512)} %bitcast.11) | data formatting | bytes 4096
  100.7 1.9 %copy.17 = bf16[128,2048]{1,0:T(8,128)(2,1)} copy(bf16[128,2048]{1,0:T(8,128)(2,1)} %get-tuple-element.14) | data formatting | bytes 1048576

commit v4 on v3

--- a/solution.py
+++ b/solution.py
@@ -91,8 +91,7 @@
     embed_hbm,
     state_hbm,
     table_hbm,
-    log_prob_ref,
-    normalizer_ref,
+    stats_ref,
     next_hbm,
     rows_all,
     weight,
@@ -276,13 +275,22 @@
         push(piece, piece, receive, (section, tensor + 2), (place <= z) & (z < 3))
         push(piece, piece, receive, (section, tensor - 2), (place >= z) & (z > 0))
 
+    middle, outer = mirrored == 1, mirrored == 0
+
+    def whole_there(step, when=None):
+        block = section * 4 + order[step]
+        wait = functools.partial(arrived, rows_all.at[block], recv_sems.at[block, 0])
+        if when is None:
+            wait()
+        else:
+            pl.when(when)(wait)
+
+    def pass_whole(step):
+        block = section * 4 + order[step]
+        along(rows_all.at[block], recv_sems.at[block, 0], order[step])
+
     def from_line(step):
-        place = order[step]
-        block = section * 4 + place
-        whole = rows_all.at[block]
-        if step:
-            arrived(whole, recv_sems.at[block, 0])
-        along(whole, recv_sems.at[block, 0], place)
+        block = section * 4 + order[step]
         for peer, parts_in_order in ((beside_x, (0, 1)), (beside_y, (1, 0))):
             for part in parts_in_order:
                 piece = rows_all.at[block, halves(step)[part]]
@@ -293,13 +301,18 @@
         weights_there(step)
         multiply(section, step)
 
-    def tails(sources, step):
+    def tails(sources, step, when=None):
         for source in sources:
             block = source * 4 + order[step]
             piece = rows_all.at[block, tail]
             if step:
-                arrived(piece, recv_sems.at[block, 2])
-            along(piece, recv_sems.at[block, 2], order[step])
+                wait = functools.partial(arrived, piece, recv_sems.at[block, 2])
+                if when is None:
+                    wait()
+                else:
+                    pl.when(when)(wait)
+            if when is not outer:
+                along(piece, recv_sems.at[block, 2], order[step])
 
     def from_beside(step):
         for source, onward, part in ((beside_x, beside_y, 0), (beside_y, beside_x, 1)):
@@ -325,18 +338,29 @@
         multiply(across, step)
 
     others = (beside_x, beside_y, across)
+    pass_whole(0)
     from_line(0)
+    whole_there(1)
+    pass_whole(1)
+    from_line(1)
+    whole_there(2, middle)
+    pass_whole(2)
     from_beside(0)
-    from_line(1)
+    whole_there(2, outer)
+    from_line(2)
     from_across(0)
-    from_line(2)
+    whole_there(3, middle)
+    pass_whole(3)
     tails(others, 1)
+    tails(others, 2, middle)
     from_beside(1)
+    whole_there(3, outer)
     from_line(3)
-    tails(others, 2)
+    tails(others, 3, middle)
     from_across(1)
+    tails(others, 2, outer)
     from_beside(2)
-    tails(others, 3)
+    tails(others, 3, outer)
     from_across(2)
     from_beside(3)
     from_across(3)
@@ -389,9 +413,7 @@
         peer_z = (z + k) % 4
         arrived(line_stats.at[peer_z], line_stat_sems.at[peer_z])
     largest, terms, chosen = combined(line_stats)
-    normalizer = largest + jnp.log(terms)
-    normalizer_ref[...] = normalizer
-    log_prob_ref[...] = chosen - normalizer
+    stats_ref[...] = packed(largest + jnp.log(terms), chosen, chosen)
 
     arrived(next_hbm, next_sem)
     for copy in unconditional:
@@ -415,15 +437,14 @@
     row_count = tile_count.shape[0]
     columns = head_weight.shape[1]
     dma = pltpu.SemaphoreType.DMA
-    log_prob, normalizer, next_input = pl.pallas_call(
+    stats, next_input = pl.pallas_call(
         head_kernel,
         out_shape=(
-            jax.ShapeDtypeStruct((1, row_count), jnp.float32),
-            jax.ShapeDtypeStruct((1, row_count), jnp.float32),
+            jax.ShapeDtypeStruct((8, row_count), jnp.float32),
             jax.ShapeDtypeStruct(chosen_embed.shape, jnp.bfloat16),
         ),
         in_specs=[HBM] * 9,
-        out_specs=(VMEM, VMEM, ANY),
+        out_specs=(VMEM, ANY),
         scratch_shapes=[
             pltpu.VMEM((16, height, width), jnp.bfloat16),
             pltpu.VMEM((4, width, columns), jnp.bfloat16),
@@ -469,7 +490,7 @@
         stack_state[None, :],
         state_table,
     )
-    return (log_prob[0], normalizer[0], next_input)
+    return (stats[1] - stats[0], stats[0], next_input)
 
 
 def solution(mesh):

time: 103 us -> 99 us (0.961)
  Pallas kernels: 97.5 us -> 94.7 us
  local copies, waits for them, and re-layouts: 4.38 us -> 2.68 us
    pallas_call x1, Pallas kernels: 97.5 us -> 94.7 us  [block_shards(): pl.pallas_call(head_kernel, out_shape=(jax.ShapeDtypeStruct((8, row_count...]
    unnamed x3, local copies, waits for them, and re-layouts: 4.38 us -> 1.88 us
where the time goes in v4:
time: 99 us; the launch traced here: 98.6 us
  Pallas kernels  94.7 us (96%)
  local copies, waits for them, and re-layouts  2.68 us (3%)
    pallas_call x1, Pallas kernels, block_shards(): pl.pallas_call(head_kernel, out_shape=(jax.ShapeDtypeStruct((8, row_count...  94.7 us

profile of v4, /device:TPU:0, one launch (start us, length us, event | category | flops | bytes accessed | tf_op | source)
XLA Modules:
  0.0 98.6 jit_solution(3813761237371769301)
XLA Ops:
  0.6 94.7 %masked_head.1 = (f32[8,512]{1,0:T(8,128)}, bf16[128,2048]{1,0:T(8,128)(2,1)}) custom-call(bf16[128,2048]{1,0:T(8,128)(2,1)} %hidden_hbm.1, f32[1,2048]{1,0:T(1,128)} %bitcast.8, bf16[16384,256]{1,0:T(8,128)(2,1)} %weight_hbm.1, s32[16,512]{1,0:T(8,128)} %bitcast.7, s32[1,512]{1,0:T(1,128)} %bitcast.12, s32[1,512]{1,0:T(1,128)} %bitcast.13, ...), custom_call_target="tpu_custom_call" | custom-call | tf_op jit(solution)/shard_map/masked_head/pallas_call | solution.py:440
  95.4 0.8 fusion
  96.2 0.0 copy-start
  96.2 0.6 sub.3
  96.8 1.9 %copy.13 = bf16[128,2048]{1,0:T(8,128)(2,1)} copy(bf16[128,2048]{1,0:T(8,128)(2,1)} %get-tuple-element.14) | data formatting | bytes 1048576
  98.6 0.0 copy-done
Async XLA Ops:
  96.2 2.5 %copy-start = (f32[1,512]{1,0:T(1,128)}, f32[1,512]{1,0:T(1,128)S(1)}, u32[]{:S(2)}) copy-start(f32[1,512]{1,0:T(1,128)S(1)} %get-tuple-element.7) | copy-start | bytes 6148

commit v5 on v4

--- a/solution.py
+++ b/solution.py
@@ -99,11 +99,11 @@
     total,
     twin_total,
     from_twin,
-    hidden,
     embed,
     table,
     merged,
-    gain_ref,
+    gains,
+    factors,
     tiles_ref,
     count_ref,
     token_ref,
@@ -116,6 +116,8 @@
     recv_sems,
     weight_sems,
     total_sems,
+    gain_sems,
+    factor_sems,
     next_sem,
     parts_sems,
     plane_sems,
@@ -131,20 +133,23 @@
     beside_x = section + 1 - 2 * x
     beside_y = section + 2 - 4 * y
     across = 3 - section
+    others = (beside_x, beside_y, across)
     twin = tensor + 1 - 2 * core
-    height, width = hidden.shape
+    height, width = embed.shape
     columns = weight.shape[2]
     device = section * tensors + tensor
+
+    own = section * 4 + z
 
     reads = [
         pltpu.make_async_copy(source, target, local_sems.at[n])
         for n, (source, target) in enumerate(
             (
-                (hidden_hbm, hidden),
+                (hidden_hbm, rows_all.at[own]),
                 (table_hbm, table),
                 (embed_hbm, embed),
                 (state_hbm, state_ref),
-                (gain_hbm, gain_ref),
+                (gain_hbm, gains.at[z]),
                 (tiles_hbm, tiles_ref),
                 (count_hbm, count_ref),
                 (token_hbm, token_ref),
@@ -177,7 +182,7 @@
         pl.semaphore_signal(barrier, inc=1, device_id=peer, device_id_type=MESH)
 
     reads[0].wait()
-    widened = hidden[...].astype(jnp.float32)
+    widened = rows_all[own].astype(jnp.float32)
     squares = jnp.sum(widened * widened, axis=1, keepdims=True)
     laid = jnp.transpose(jnp.broadcast_to(squares, (height, 128)))[0:8, :]
     parts[pl.ds(tensor, 1)] = laid[None]
@@ -227,6 +232,34 @@
 
     for peer in line:
         push(parts.at[tensor], parts.at[tensor], parts_sems.at[tensor], peer)
+    reads[4].wait()
+    for k in range(1, 4):
+        push(gains.at[z], gains.at[z], gain_sems.at[z], (section, ((z + k) % 4) * 2 + core))
+
+    first = height * 3 // 4
+    tail = pl.ds(first, height - first)
+
+    def halves(step):
+        size = (first if step else height) // 2
+        return pl.ds(0, size), pl.ds(size, size)
+
+    def along(piece, receive, place):
+        push(piece, piece, receive, (section, tensor + 2), (place <= z) & (z < 3))
+        push(piece, piece, receive, (section, tensor - 2), (place >= z) & (z > 0))
+
+    def pass_whole(step):
+        block = section * 4 + order[step]
+        along(rows_all.at[block], recv_sems.at[block, 0], order[step])
+
+    def send_round(step):
+        block = section * 4 + order[step]
+        for peer, parts_in_order in ((beside_x, (0, 1)), (beside_y, (1, 0))):
+            for part in parts_in_order:
+                piece = rows_all.at[block, halves(step)[part]]
+                push(piece, piece, recv_sems.at[block, part], (peer, tensor))
+
+    pass_whole(0)
+    send_round(0)
 
     reads[3].wait()
     states = lax.broadcasted_iota(jnp.int32, (table.shape[0], height), 0)
@@ -239,41 +272,35 @@
 
     send_weight(0)
 
+    for step in range(1, 4):
+        send_weight(step)
+
     for _, peer in line:
         arrived(parts.at[peer], parts_sems.at[peer])
-    squares_total = jnp.sum(parts[...], axis=0)[0:1, :]
-    reads[4].wait()
-    factor = lax.rsqrt(squares_total / (width * tensors) + EPSILON)
-    factor = jnp.transpose(jnp.broadcast_to(factor, (128, height)))[:, 0:1]
-    own = section * 4 + z
-    rows_all[pl.ds(own, 1)] = (hidden[...].astype(jnp.float32) * factor * gain_ref[...]).astype(jnp.bfloat16)[None]
-
-    first = height * 3 // 4
-    tail = pl.ds(first, height - first)
-
-    def halves(step):
-        size = (first if step else height) // 2
-        return pl.ds(0, size), pl.ds(size, size)
+    squares_total = jnp.sum(parts[...], axis=0)
+    factors[pl.ds(section, 1)] = lax.rsqrt(squares_total / (width * tensors) + EPSILON)[None]
+    for peer in others:
+        push(factors.at[section], factors.at[section], factor_sems.at[section], (peer, tensor))
 
     def multiply(source, step):
         place = order[step]
         row = pl.ds(pl.multiple_of(source * height, height), height)
-        block = rows_all[source * 4 + place]
+        if step == 0 and source is not section:
+            arrived(factors.at[source], factor_sems.at[source])
+        factor = jnp.transpose(jnp.broadcast_to(factors[source][0:1, :], (height, height)))[:, 0:1]
+        widened = rows_all[source * 4 + place].astype(jnp.float32)
+        block = (widened * factor * gains[place]).astype(jnp.bfloat16)
         for sums, by in ((twin_total, twin_weight), (total, weight)):
             product = jnp.dot(block, by[place], preferred_element_type=jnp.float32)
             if step:
                 product += sums[row, :]
             sums[row, :] = product
-        if step == 3:
-            push(twin_total.at[row], from_twin.at[row], total_sems.at[source], (section, twin))
+            if step == 3 and sums is twin_total:
+                push(twin_total.at[row], from_twin.at[row], total_sems.at[source], (section, twin))
 
     def weights_there(step):
         weight_reads[step].wait()
         arrived(twin_weight.at[order[step]], weight_sems.at[order[step]])
-
-    def along(piece, receive, place):
-        push(piece, piece, receive, (section, tensor + 2), (place <= z) & (z < 3))
-        push(piece, piece, receive, (section, tensor - 2), (place >= z) & (z > 0))
 
     middle, outer = mirrored == 1, mirrored == 0
 
@@ -285,19 +312,10 @@
         else:
             pl.when(when)(wait)
 
-    def pass_whole(step):
-        block = section * 4 + order[step]
-        along(rows_all.at[block], recv_sems.at[block, 0], order[step])
-
     def from_line(step):
-        block = section * 4 + order[step]
-        for peer, parts_in_order in ((beside_x, (0, 1)), (beside_y, (1, 0))):
-            for part in parts_in_order:
-                piece = rows_all.at[block, halves(step)[part]]
-                push(piece, piece, recv_sems.at[block, part], (peer, tensor))
-        if step == 0:
-            for later in range(1, 4):
-                send_weight(later)
+        if step:
+            send_round(step)
+            arrived(gains.at[order[step]], gain_sems.at[order[step]])
         weights_there(step)
         multiply(section, step)
 
@@ -337,8 +355,6 @@
             tails((across,), 0)
         multiply(across, step)
 
-    others = (beside_x, beside_y, across)
-    pass_whole(0)
     from_line(0)
     whole_there(1)
     pass_whole(1)
@@ -452,11 +468,11 @@
             pltpu.VMEM((row_count, columns), jnp.float32),
             pltpu.VMEM((row_count, columns), jnp.float32),
             pltpu.VMEM((row_count, columns), jnp.float32),
-            pltpu.VMEM(hidden.shape, jnp.bfloat16),
             pltpu.VMEM(chosen_embed.shape, jnp.bfloat16),
             pltpu.VMEM(state_table.shape, jnp.bfloat16),
             pltpu.VMEM(chosen_embed.shape, jnp.bfloat16),
-            pltpu.VMEM((1, width), jnp.float32),
+            pltpu.VMEM((4, 1, width), jnp.float32),
+            pltpu.VMEM((4, 8, height), jnp.float32),
             pltpu.VMEM(tile_list.shape[::-1], jnp.int32),
             pltpu.VMEM((1, row_count), jnp.int32),
             pltpu.VMEM((1, row_count), jnp.int32),
@@ -467,6 +483,8 @@
             dma((80,)),
             dma((32,)),
             dma((16, 3)),
+            dma((4,)),
+            dma((4,)),
             dma((4,)),
             dma((4,)),
             dma,

time: 99 us -> 99 us (level)
  no operation moved by 1% of the time
where the time goes in v5:
time: 99 us; the launch traced here: 98.7 us
  Pallas kernels  94.8 us (96%)
  local copies, waits for them, and re-layouts  2.68 us (3%)
    pallas_call x1, Pallas kernels, block_shards(): pl.pallas_call(head_kernel, out_shape=(jax.ShapeDtypeStruct((8, row_count...  94.8 us

profile of v5, /device:TPU:0, one launch (start us, length us, event | category | flops | bytes accessed | tf_op | source)
XLA Modules:
  0.0 98.7 jit_solution(15780097298633481929)
XLA Ops:
  0.6 94.8 %masked_head.1 = (f32[8,512]{1,0:T(8,128)}, bf16[128,2048]{1,0:T(8,128)(2,1)}) custom-call(bf16[128,2048]{1,0:T(8,128)(2,1)} %hidden_hbm.1, f32[1,2048]{1,0:T(1,128)} %bitcast.8, bf16[16384,256]{1,0:T(8,128)(2,1)} %weight_hbm.1, s32[16,512]{1,0:T(8,128)} %bitcast.7, s32[1,512]{1,0:T(1,128)} %bitcast.12, s32[1,512]{1,0:T(1,128)} %bitcast.13, ...), custom_call_target="tpu_custom_call" | custom-call | tf_op jit(solution)/shard_map/masked_head/pallas_call | solution.py:456
  95.4 0.8 fusion
  96.2 0.0 copy-start
  96.2 0.6 sub.3
  96.8 1.9 %copy.13 = bf16[128,2048]{1,0:T(8,128)(2,1)} copy(bf16[128,2048]{1,0:T(8,128)(2,1)} %get-tuple-element.14) | data formatting | bytes 1048576
  98.7 0.0 copy-done
Async XLA Ops:
  96.2 2.5 %copy-start = (f32[1,512]{1,0:T(1,128)}, f32[1,512]{1,0:T(1,128)S(1)}, u32[]{:S(2)}) copy-start(f32[1,512]{1,0:T(1,128)S(1)} %get-tuple-element.7) | copy-start | bytes 6148

commit v6 on v5

--- a/solution.py
+++ b/solution.py
@@ -243,9 +243,14 @@
         size = (first if step else height) // 2
         return pl.ds(0, size), pl.ds(size, size)
 
-    def along(piece, receive, place):
-        push(piece, piece, receive, (section, tensor + 2), (place <= z) & (z < 3))
-        push(piece, piece, receive, (section, tensor - 2), (place >= z) & (z > 0))
+    middle, outer = mirrored == 1, mirrored == 0
+
+    def along(piece, receive, place, there=None):
+        up, down = (place <= z) & (z < 3), (place >= z) & (z > 0)
+        if there is not None:
+            up, down = up & there, down & there
+        push(piece, piece, receive, (section, tensor + 2), up)
+        push(piece, piece, receive, (section, tensor - 2), down)
 
     def pass_whole(step):
         block = section * 4 + order[step]
@@ -302,8 +307,6 @@
         weight_reads[step].wait()
         arrived(twin_weight.at[order[step]], weight_sems.at[order[step]])
 
-    middle, outer = mirrored == 1, mirrored == 0
-
     def whole_there(step, when=None):
         block = section * 4 + order[step]
         wait = functools.partial(arrived, rows_all.at[block], recv_sems.at[block, 0])
@@ -329,8 +332,8 @@
                     wait()
                 else:
                     pl.when(when)(wait)
-            if when is not outer:
-                along(piece, recv_sems.at[block, 2], order[step])
+            if when is not outer or step == 0:
+                along(piece, recv_sems.at[block, 2], order[step], when)
 
     def from_beside(step):
         for source, onward, part in ((beside_x, beside_y, 0), (beside_y, beside_x, 1)):
@@ -343,7 +346,7 @@
             piece = rows_all.at[block, halves(step)[part]]
             arrived(piece, recv_sems.at[block, part])
             if step == 0:
-                tails((source,), 0)
+                tails((source,), 0, outer)
         multiply(beside_x, step)
         multiply(beside_y, step)
 
@@ -352,7 +355,7 @@
         for part in range(2):
             arrived(rows_all.at[block, halves(step)[part]], recv_sems.at[block, part])
         if step == 0:
-            tails((across,), 0)
+            tails((across,), 0, outer)
         multiply(across, step)
 
     from_line(0)
@@ -364,9 +367,10 @@
     from_beside(0)
     whole_there(2, outer)
     from_line(2)
-    from_across(0)
     whole_there(3, middle)
     pass_whole(3)
+    from_across(0)
+    tails(others, 0, middle)
     tails(others, 1)
     tails(others, 2, middle)
     from_beside(1)
@@ -481,7 +485,7 @@
             pltpu.VMEM((8, 8, row_count), jnp.float32),
             pltpu.VMEM((4, 8, row_count), jnp.float32),
             dma((80,)),
-            dma((32,)),
+            dma((40,)),
             dma((16, 3)),
             dma((4,)),
             dma((4,)),

time: 99 us -> 96.4 us (0.974)
  Pallas kernels: 94.8 us -> 92.2 us
    pallas_call x1, Pallas kernels: 94.8 us -> 92.2 us  [block_shards(): pl.pallas_call(head_kernel, out_shape=(jax.ShapeDtypeStruct((8, row_count...]
where the time goes in v6:
time: 96.4 us; the launch traced here: 96.1 us
  Pallas kernels  92.2 us (96%)
  local copies, waits for them, and re-layouts  2.68 us (3%)
    pallas_call x1, Pallas kernels, block_shards(): pl.pallas_call(head_kernel, out_shape=(jax.ShapeDtypeStruct((8, row_count...  92.2 us

profile of v6, /device:TPU:0, one launch (start us, length us, event | category | flops | bytes accessed | tf_op | source)
XLA Modules:
  0.0 96.1 jit_solution(3544364500300081896)
XLA Ops:
  0.6 92.2 %masked_head.1 = (f32[8,512]{1,0:T(8,128)}, bf16[128,2048]{1,0:T(8,128)(2,1)}) custom-call(bf16[128,2048]{1,0:T(8,128)(2,1)} %hidden_hbm.1, f32[1,2048]{1,0:T(1,128)} %bitcast.8, bf16[16384,256]{1,0:T(8,128)(2,1)} %weight_hbm.1, s32[16,512]{1,0:T(8,128)} %bitcast.7, s32[1,512]{1,0:T(1,128)} %bitcast.12, s32[1,512]{1,0:T(1,128)} %bitcast.13, ...), custom_call_target="tpu_custom_call" | custom-call | tf_op jit(solution)/shard_map/masked_head/pallas_call | solution.py:460
  92.8 0.8 fusion
  93.6 0.0 copy-start
  93.7 0.6 sub.3
  94.2 1.9 %copy.13 = bf16[128,2048]{1,0:T(8,128)(2,1)} copy(bf16[128,2048]{1,0:T(8,128)(2,1)} %get-tuple-element.14) | data formatting | bytes 1048576
  96.1 0.0 copy-done
Async XLA Ops:
  93.6 2.5 %copy-start = (f32[1,512]{1,0:T(1,128)}, f32[1,512]{1,0:T(1,128)S(1)}, u32[]{:S(2)}) copy-start(f32[1,512]{1,0:T(1,128)S(1)} %get-tuple-element.7) | copy-start | bytes 6148
